TPU v7x, 32 devices: a whole 2x2x4 slice. The times are simulated.
32 devices in a mesh: dp: 8 (over z, x), pipe: 4 (over y, core).
Axes of the slice: x: 2, y: 2, z: 4, core: 2. Of those that a mesh axis runs over, the one named last changes fastest.
Arguments:
- tokens: bfloat16 [64, 64, 3072], P('dp'), may hold values from -40 to 40
- segments: int32 [64, 64], P('dp'), may hold values from 0 to 5, never falling along the last dimension, each value on 1 to 24 neighbouring positions
- keep_mask: int32 [64, 64], P('dp'), may hold values 0 or 1
- norm_gain: float32 [4, 3072], P('pipe'), may hold values from 0.5 to 2
- norm_bias: float32 [4, 3072], P('pipe'), may hold values from -3 to 3
- w_qkv: bfloat16 [4, 3072, 4608], P('pipe', 'dp'), may hold values from -0.109375 to 0.109375
- w_out: bfloat16 [4, 1536, 3072], P('pipe', 'dp'), may hold values from -0.15625 to 0.15625
Outputs:
- layer_outputs: bfloat16 [4, 64, 64, 3072], P('pipe', 'dp')
Inputs may be any that keep to these rules, and one draw needn't show every extreme that they name: `segments`: image numbers never fall along a sequence; every image spans 1 to 24 patches and one spans exactly 24.
All inputs are finite; a program needn't handle non-finite values. No bound on the sum of `keep_mask` on one device may be relied on, other than what follows from the above.
Results may differ from a plain program's by a relative error of at most 0.013.
Values may be sent and summed in bfloat16 or wider, within the bound.
A program may use at most 128 MiB of HBM per device.

v0:
```python
import math

import jax
import jax.numpy as jnp
from jax import lax
from jax.sharding import PartitionSpec as P

D = 3072
HEADS = 24
HD = 64
GROUPS = 32
IMGS = 6
INNER = 1536


norm_eps = 1e-05


def passed_along(value, axis, steps):
    count = lax.axis_size(axis)
    first, last = (max(0, -steps), min(count, count - steps))
    return lax.ppermute(value, axis, [(source, source + steps) for source in range(first, last)])


def group_normed(stream, seg_row, keep_row, gain, bias_row):
    length = stream.shape[0]
    group_width = D // GROUPS
    values = stream.astype(jnp.float32).reshape(length, GROUPS, group_width)
    member = (
        (seg_row[:, None] == jnp.arange(IMGS, dtype=jnp.int32)[None, :]) & (keep_row[:, None] > 0)
    ).astype(jnp.float32)
    counted = jnp.maximum(jnp.sum(member, axis=0) * group_width, 1.0)
    img_sum = jnp.dot(member.T, jnp.sum(values, axis=2), precision=lax.Precision.HIGHEST)
    img_mean = img_sum / counted[:, None]
    tok_mean = jnp.dot(member, img_mean, precision=lax.Precision.HIGHEST)
    centred = values - tok_mean[:, :, None]
    img_var = (
        jnp.dot(member.T, jnp.sum(centred * centred, axis=2), precision=lax.Precision.HIGHEST)
        / counted[:, None]
    )
    tok_var = jnp.dot(member, img_var, precision=lax.Precision.HIGHEST)
    normed = (centred * lax.rsqrt(tok_var + norm_eps)[:, :, None]).reshape(length, D)
    normed = (normed * gain[None, :] + bias_row[None, :]) * keep_row[:, None].astype(jnp.float32)
    return normed.astype(jnp.bfloat16)


def attend(stream, seg_row, keep_row, gain, bias_row, qkv_weight):
    length = stream.shape[0]
    normed = group_normed(stream, seg_row, keep_row, gain, bias_row)
    projected = jnp.dot(normed, qkv_weight, preferred_element_type=jnp.float32)
    query_rows = projected[:, :INNER].reshape(length, HEADS, HD)
    key_rows = projected[:, INNER : 2 * INNER].reshape(length, HEADS, HD)
    value_rows = projected[:, 2 * INNER :].reshape(length, HEADS, HD).astype(jnp.bfloat16)
    query_rows = (
        query_rows * lax.rsqrt(jnp.mean(query_rows * query_rows, axis=2, keepdims=True) + 1e-06)
    ).astype(jnp.bfloat16)
    key_rows = (
        key_rows * lax.rsqrt(jnp.mean(key_rows * key_rows, axis=2, keepdims=True) + 1e-06)
    ).astype(jnp.bfloat16)
    scores = jnp.einsum(
        "qhd,khd->hqk", query_rows, key_rows, preferred_element_type=jnp.float32
    ) / math.sqrt(HD)
    keep_float = keep_row.astype(jnp.float32)
    allowed = (
        (seg_row[:, None] == seg_row[None, :]).astype(jnp.float32)
        * keep_float[:, None]
        * keep_float[None, :]
    )
    expo = jnp.exp(scores) * allowed[None, :, :]
    denominator = jnp.sum(expo, axis=2) + (1.0 - keep_float)[None, :]
    probs = (expo / denominator[:, :, None]).astype(jnp.bfloat16)
    attended = jnp.einsum("hqk,khd->qhd", probs, value_rows, preferred_element_type=jnp.float32)
    return attended.reshape(length, INNER).astype(jnp.bfloat16)


def finish(stream, attended, out_weight):
    branch = jnp.dot(attended, out_weight, preferred_element_type=jnp.float32)
    return (stream.astype(jnp.float32) + branch).astype(jnp.bfloat16)


def advance(stream):
    return passed_along(stream, "pipe", 1)


def local(tokens, segments, keep_mask, norm_gain, norm_bias, w_qkv, w_out):
    section_no = lax.axis_index("pipe")
    sections = lax.axis_size("pipe")
    micro = tokens.shape[0]
    gain = norm_gain[0]
    bias_row = norm_bias[0]
    saved = jnp.zeros((1,) + tokens.shape, jnp.bfloat16)

    def store(saved, result, micro_idx):
        is_live = (micro_idx >= 0) & (micro_idx < micro)
        clipped = jnp.clip(micro_idx, 0, micro - 1)
        kept = jnp.where(is_live, result, saved[0, clipped])
        return lax.dynamic_update_slice(saved, kept[None, None], (0, clipped, 0, 0))

    incoming = jnp.zeros(tokens.shape[1:], jnp.bfloat16)
    qkv_all = lax.all_gather(w_qkv, "dp", axis=1, tiled=True)
    qkv_full = qkv_all[0]
    section_input = jnp.where(section_no == 0, tokens[0], incoming)
    attended = attend(section_input, segments[0], keep_mask[0], gain, bias_row, qkv_full)
    shard_rows = lax.all_gather(w_out, "dp", axis=1, tiled=True)
    branch_sum = jnp.dot(attended, shard_rows[0], preferred_element_type=jnp.float32)
    out_buffer = shard_rows
    branch_sum, out_buffer = (branch_sum, out_buffer)
    result = (section_input.astype(jnp.float32) + branch_sum).astype(jnp.bfloat16)
    saved = store(saved, result, 0 - section_no)
    state = (advance(result), saved)
    out_full = out_buffer[0]

    def tick(tick_no, running):
        incoming, saved_now = running
        micro_idx = tick_no - section_no
        is_live = (micro_idx >= 0) & (micro_idx < micro)
        clipped = jnp.clip(micro_idx, 0, micro - 1)
        section_input = jnp.where(section_no == 0, tokens[clipped], incoming)
        seg_row = segments[clipped]
        keep_row = keep_mask[clipped]

        def compute(stream):
            return finish(
                stream, attend(stream, seg_row, keep_row, gain, bias_row, qkv_full), out_full
            )

        def pass_on(stream):
            return stream

        result = lax.cond(is_live, compute, pass_on, section_input)
        saved_now = store(saved_now, result, micro_idx)
        return (advance(result), saved_now)

    final_state = lax.fori_loop(1, micro + sections - 1, tick, state)
    return final_state[1]


def solution(mesh):
    placed = (
        P("dp", None, None),
        P("dp", None),
        P("dp", None),
        P("pipe", None),
        P("pipe", None),
        P("pipe", "dp", None),
        P("pipe", "dp", None),
    )
    return jax.shard_map(
        local, mesh=mesh, in_specs=placed, out_specs=P("pipe", "dp", None, None), check_vma=False
    )
```

profile of v0, /device:TPU:4, one launch (start us, length us, event | category | flops | bytes accessed | tf_op | source)
XLA Modules:
  0.0 1069.3 jit_solution(9755468899693381160)
XLA Ops:
  8.0 1.1 select_convert_fusion
  15.8 533.7 %all-gather.3.cloned.1.call-done = bf16[1,3072,4608]{2,1,0:T(8,128)(2,1)} async-done(((bf16[1,384,4608]{2,1,0:T(8,128)(2,1)}), bf16[1,3072,4608]{2,1,0:T(8,128)(2,1)}) %all-gather.3.cloned.1.call-update) | async-done | bytes 28311568 | tf_op jit(solution)/shard_map/all_gather | solution.py:100
  549.5 11.6 %fusion.48 = f32[64,4608]{1,0:T(8,128)S(1)} fusion(bf16[64,3072]{1,0:T(8,128)(2,1)S(1)} %convert_element_type.170, bf16[1,3072,4608]{2,1,0:T(8,128)(2,1)} %all-gather.3.cloned.1.call-done), kind=kOutput, calls=%fused_computation.97 | convolution fusion | flops 1811939328 | bytes 29884416 | tf_op jit(solution)/shard_map/dot_general | solution.py:50
  563.6 126.2 %all-gather.5.cloned.1.call-done = bf16[1,1536,3072]{2,1,0:T(8,128)(2,1)} async-done(((bf16[1,192,3072]{2,1,0:T(8,128)(2,1)}), bf16[1,1536,3072]{2,1,0:T(8,128)(2,1)}) %all-gather.5.cloned.1.call-update) | async-done | bytes 9437200 | tf_op jit(solution)/shard_map/all_gather | solution.py:104
  690.2 5.5 bitcast_dynamic-update-slice_fusion.1
  695.7 1.7 copy-done.1
  697.3 2.1 collective-permute-start.1
  699.4 7.0 collective-permute-done.1
  706.4 356.0 %while.16 = (s32[]{:T(128)}, bf16[64,3072]{1,0:T(8,128)(2,1)S(1)}, bf16[1,8,64,3072]{3,2,1,0:T(8,128)(2,1)}, s32[]{:T(128)}, pred[]{:T(512)}, /*index=5*/bf16[8,...) while((s32[]{:T(128)}, bf16[64,3072]{1,0:T(8,128)(2,1)S(1)}, ...), condition=%wide.region_15.16_spmd, body=%wide.region_6.15_spmd.sunk | while | flops 2446215168 | bytes 66486384 | solution.py:134
  706.4 1.0 bitcast_select_fusion.3
  707.5 1.9 collective-permute-start
  709.4 1.0 constant_dynamic-slice_fusion.3
  711.3 29.6 %collective-permute-done = bf16[64,3072]{1,0:T(8,128)(2,1)S(1)} collective-permute-done((bf16[64,3072]{1,0:T(8,128)(2,1)S(1)}, bf16[64,3072]{1,0:T(8,128)(2,1)S(1)}, u32[]{:S(2)}, u32[]{:S(2)}) %collective-permute-start) | collective-permute-done | bytes 393248 | tf_op jit(solution)/shard_map/while/body/eval_jaxpr/ppermute | solution.py:22
  740.9 1.0 bitcast_select_fusion.3
  741.9 26.8 %conditional.2 = (bf16[64,3072]{1,0:T(8,128)(2,1)S(1)}) conditional(s32[]{:T(128)} %convert_element_type.211, bf16[64,3072]{1,0:T(8,128)(2,1)S(1)} %bitcast_select_fusion.3, (bf16[64,3072]{1,0:T(8,128)(2,1)S(1)}, s32[8,64]{1,0:T(8,128)}, s32[]{:T(128)}, s32[8,64]{1,0:T(8,128)S(1)}, f32[1,3072]{1,0:T(1,128)S(1)}, /*index=5*/f32[1,3072]{1,0:T(1,128)S(1)}, ...), branch_computations={%region_7.7_spmd, %region_8.14_spmd} | conditional | flops 2445821952 | bytes 61766956 | solution.py:130
  747.0 11.7 %fusion.4 = f32[64,4608]{1,0:T(8,128)S(1)} fusion(bf16[3072,4608]{1,0:T(8,128)(2,1)} %get-tuple-element.298, f32[64,3072]{1,0:T(8,128)S(1)} %mul.195, f32[64,3072]{1,0:T(8,128)S(1)} %sub.48, f32[64]{0:T(128)S(1)} %get-tuple-element.340, f32[3072]{0:T(1024)S(1)} %bitcast.70, f32[3072]{0:T(1024)S(1)} %bitcast.71, bf16[64,3072]{1,0:T(8,128)(2,1)S(1)} %get-tuple-element.292), kind=kOutput, calls=%fused_computation.17 | convolution fusion | flops 1813315584 | bytes 31482112 | tf_op jit(solution)/shard_map/while/body/eval_jaxpr/cond/branch_1_fun/dot_general | solution.py:50
  763.2 5.5 fusion
  768.7 1.9 collective-permute-start
  770.6 1.0 constant_dynamic-slice_fusion.3
  772.5 5.3 collective-permute-done
  777.8 1.0 bitcast_select_fusion.3
  778.9 26.8 %conditional.2 = (bf16[64,3072]{1,0:T(8,128)(2,1)S(1)}) conditional(s32[]{:T(128)} %convert_element_type.211, bf16[64,3072]{1,0:T(8,128)(2,1)S(1)} %bitcast_select_fusion.3, (bf16[64,3072]{1,0:T(8,128)(2,1)S(1)}, s32[8,64]{1,0:T(8,128)}, s32[]{:T(128)}, s32[8,64]{1,0:T(8,128)S(1)}, f32[1,3072]{1,0:T(1,128)S(1)}, /*index=5*/f32[1,3072]{1,0:T(1,128)S(1)}, ...), branch_computations={%region_7.7_spmd, %region_8.14_spmd} | conditional | flops 2445821952 | bytes 61766956 | solution.py:130
  783.9 11.7 %fusion.4 = f32[64,4608]{1,0:T(8,128)S(1)} fusion(bf16[3072,4608]{1,0:T(8,128)(2,1)} %get-tuple-element.298, f32[64,3072]{1,0:T(8,128)S(1)} %mul.195, f32[64,3072]{1,0:T(8,128)S(1)} %sub.48, f32[64]{0:T(128)S(1)} %get-tuple-element.340, f32[3072]{0:T(1024)S(1)} %bitcast.70, f32[3072]{0:T(1024)S(1)} %bitcast.71, bf16[64,3072]{1,0:T(8,128)(2,1)S(1)} %get-tuple-element.292), kind=kOutput, calls=%fused_computation.17 | convolution fusion | flops 1813315584 | bytes 31482112 | tf_op jit(solution)/shard_map/while/body/eval_jaxpr/cond/branch_1_fun/dot_general | solution.py:50
  800.1 5.5 fusion
  805.6 1.9 collective-permute-start
  809.4 5.3 collective-permute-done
  814.7 1.0 bitcast_select_fusion.3
  815.8 26.8 %conditional.2 = (bf16[64,3072]{1,0:T(8,128)(2,1)S(1)}) conditional(s32[]{:T(128)} %convert_element_type.211, bf16[64,3072]{1,0:T(8,128)(2,1)S(1)} %bitcast_select_fusion.3, (bf16[64,3072]{1,0:T(8,128)(2,1)S(1)}, s32[8,64]{1,0:T(8,128)}, s32[]{:T(128)}, s32[8,64]{1,0:T(8,128)S(1)}, f32[1,3072]{1,0:T(1,128)S(1)}, /*index=5*/f32[1,3072]{1,0:T(1,128)S(1)}, ...), branch_computations={%region_7.7_spmd, %region_8.14_spmd} | conditional | flops 2445821952 | bytes 61766956 | solution.py:130
  820.9 11.7 %fusion.4 = f32[64,4608]{1,0:T(8,128)S(1)} fusion(bf16[3072,4608]{1,0:T(8,128)(2,1)} %get-tuple-element.298, f32[64,3072]{1,0:T(8,128)S(1)} %mul.195, f32[64,3072]{1,0:T(8,128)S(1)} %sub.48, f32[64]{0:T(128)S(1)} %get-tuple-element.340, f32[3072]{0:T(1024)S(1)} %bitcast.70, f32[3072]{0:T(1024)S(1)} %bitcast.71, bf16[64,3072]{1,0:T(8,128)(2,1)S(1)} %get-tuple-element.292), kind=kOutput, calls=%fused_computation.17 | convolution fusion | flops 1813315584 | bytes 31482112 | tf_op jit(solution)/shard_map/while/body/eval_jaxpr/cond/branch_1_fun/dot_general | solution.py:50
  837.1 5.5 fusion
  842.6 1.9 collective-permute-start
  846.4 5.3 collective-permute-done
  851.7 1.0 bitcast_select_fusion.3
  852.7 26.8 %conditional.2 = (bf16[64,3072]{1,0:T(8,128)(2,1)S(1)}) conditional(s32[]{:T(128)} %convert_element_type.211, bf16[64,3072]{1,0:T(8,128)(2,1)S(1)} %bitcast_select_fusion.3, (bf16[64,3072]{1,0:T(8,128)(2,1)S(1)}, s32[8,64]{1,0:T(8,128)}, s32[]{:T(128)}, s32[8,64]{1,0:T(8,128)S(1)}, f32[1,3072]{1,0:T(1,128)S(1)}, /*index=5*/f32[1,3072]{1,0:T(1,128)S(1)}, ...), branch_computations={%region_7.7_spmd, %region_8.14_spmd} | conditional | flops 2445821952 | bytes 61766956 | solution.py:130
  857.8 11.7 %fusion.4 = f32[64,4608]{1,0:T(8,128)S(1)} fusion(bf16[3072,4608]{1,0:T(8,128)(2,1)} %get-tuple-element.298, f32[64,3072]{1,0:T(8,128)S(1)} %mul.195, f32[64,3072]{1,0:T(8,128)S(1)} %sub.48, f32[64]{0:T(128)S(1)} %get-tuple-element.340, f32[3072]{0:T(1024)S(1)} %bitcast.70, f32[3072]{0:T(1024)S(1)} %bitcast.71, bf16[64,3072]{1,0:T(8,128)(2,1)S(1)} %get-tuple-element.292), kind=kOutput, calls=%fused_computation.17 | convolution fusion | flops 1813315584 | bytes 31482112 | tf_op jit(solution)/shard_map/while/body/eval_jaxpr/cond/branch_1_fun/dot_general | solution.py:50
  874.0 5.5 fusion
  879.5 1.9 collective-permute-start
  883.3 5.3 collective-permute-done
  888.6 1.0 bitcast_select_fusion.3
  889.6 26.8 %conditional.2 = (bf16[64,3072]{1,0:T(8,128)(2,1)S(1)}) conditional(s32[]{:T(128)} %convert_element_type.211, bf16[64,3072]{1,0:T(8,128)(2,1)S(1)} %bitcast_select_fusion.3, (bf16[64,3072]{1,0:T(8,128)(2,1)S(1)}, s32[8,64]{1,0:T(8,128)}, s32[]{:T(128)}, s32[8,64]{1,0:T(8,128)S(1)}, f32[1,3072]{1,0:T(1,128)S(1)}, /*index=5*/f32[1,3072]{1,0:T(1,128)S(1)}, ...), branch_computations={%region_7.7_spmd, %region_8.14_spmd} | conditional | flops 2445821952 | bytes 61766956 | solution.py:130
  894.7 11.7 %fusion.4 = f32[64,4608]{1,0:T(8,128)S(1)} fusion(bf16[3072,4608]{1,0:T(8,128)(2,1)} %get-tuple-element.298, f32[64,3072]{1,0:T(8,128)S(1)} %mul.195, f32[64,3072]{1,0:T(8,128)S(1)} %sub.48, f32[64]{0:T(128)S(1)} %get-tuple-element.340, f32[3072]{0:T(1024)S(1)} %bitcast.70, f32[3072]{0:T(1024)S(1)} %bitcast.71, bf16[64,3072]{1,0:T(8,128)(2,1)S(1)} %get-tuple-element.292), kind=kOutput, calls=%fused_computation.17 | convolution fusion | flops 1813315584 | bytes 31482112 | tf_op jit(solution)/shard_map/while/body/eval_jaxpr/cond/branch_1_fun/dot_general | solution.py:50
  910.9 5.5 fusion
  916.4 1.9 collective-permute-start
  920.2 5.3 collective-permute-done
  925.5 1.0 bitcast_select_fusion.3
  926.6 26.8 %conditional.2 = (bf16[64,3072]{1,0:T(8,128)(2,1)S(1)}) conditional(s32[]{:T(128)} %convert_element_type.211, bf16[64,3072]{1,0:T(8,128)(2,1)S(1)} %bitcast_select_fusion.3, (bf16[64,3072]{1,0:T(8,128)(2,1)S(1)}, s32[8,64]{1,0:T(8,128)}, s32[]{:T(128)}, s32[8,64]{1,0:T(8,128)S(1)}, f32[1,3072]{1,0:T(1,128)S(1)}, /*index=5*/f32[1,3072]{1,0:T(1,128)S(1)}, ...), branch_computations={%region_7.7_spmd, %region_8.14_spmd} | conditional | flops 2445821952 | bytes 61766956 | solution.py:130
  931.6 11.7 %fusion.4 = f32[64,4608]{1,0:T(8,128)S(1)} fusion(bf16[3072,4608]{1,0:T(8,128)(2,1)} %get-tuple-element.298, f32[64,3072]{1,0:T(8,128)S(1)} %mul.195, f32[64,3072]{1,0:T(8,128)S(1)} %sub.48, f32[64]{0:T(128)S(1)} %get-tuple-element.340, f32[3072]{0:T(1024)S(1)} %bitcast.70, f32[3072]{0:T(1024)S(1)} %bitcast.71, bf16[64,3072]{1,0:T(8,128)(2,1)S(1)} %get-tuple-element.292), kind=kOutput, calls=%fused_computation.17 | convolution fusion | flops 1813315584 | bytes 31482112 | tf_op jit(solution)/shard_map/while/body/eval_jaxpr/cond/branch_1_fun/dot_general | solution.py:50
  947.8 5.5 fusion
  953.3 1.9 collective-permute-start
  957.1 5.3 collective-permute-done
  962.4 1.0 bitcast_select_fusion.3
  963.5 26.8 %conditional.2 = (bf16[64,3072]{1,0:T(8,128)(2,1)S(1)}) conditional(s32[]{:T(128)} %convert_element_type.211, bf16[64,3072]{1,0:T(8,128)(2,1)S(1)} %bitcast_select_fusion.3, (bf16[64,3072]{1,0:T(8,128)(2,1)S(1)}, s32[8,64]{1,0:T(8,128)}, s32[]{:T(128)}, s32[8,64]{1,0:T(8,128)S(1)}, f32[1,3072]{1,0:T(1,128)S(1)}, /*index=5*/f32[1,3072]{1,0:T(1,128)S(1)}, ...), branch_computations={%region_7.7_spmd, %region_8.14_spmd} | conditional | flops 2445821952 | bytes 61766956 | solution.py:130
  968.6 11.7 %fusion.4 = f32[64,4608]{1,0:T(8,128)S(1)} fusion(bf16[3072,4608]{1,0:T(8,128)(2,1)} %get-tuple-element.298, f32[64,3072]{1,0:T(8,128)S(1)} %mul.195, f32[64,3072]{1,0:T(8,128)S(1)} %sub.48, f32[64]{0:T(128)S(1)} %get-tuple-element.340, f32[3072]{0:T(1024)S(1)} %bitcast.70, f32[3072]{0:T(1024)S(1)} %bitcast.71, bf16[64,3072]{1,0:T(8,128)(2,1)S(1)} %get-tuple-element.292), kind=kOutput, calls=%fused_computation.17 | convolution fusion | flops 1813315584 | bytes 31482112 | tf_op jit(solution)/shard_map/while/body/eval_jaxpr/cond/branch_1_fun/dot_general | solution.py:50
  984.8 5.5 fusion
  990.3 1.9 collective-permute-start
  994.1 5.3 collective-permute-done
  999.4 1.0 bitcast_select_fusion.3
  1000.4 26.8 %conditional.2 = (bf16[64,3072]{1,0:T(8,128)(2,1)S(1)}) conditional(s32[]{:T(128)} %convert_element_type.211, bf16[64,3072]{1,0:T(8,128)(2,1)S(1)} %bitcast_select_fusion.3, (bf16[64,3072]{1,0:T(8,128)(2,1)S(1)}, s32[8,64]{1,0:T(8,128)}, s32[]{:T(128)}, s32[8,64]{1,0:T(8,128)S(1)}, f32[1,3072]{1,0:T(1,128)S(1)}, /*index=5*/f32[1,3072]{1,0:T(1,128)S(1)}, ...), branch_computations={%region_7.7_spmd, %region_8.14_spmd} | conditional | flops 2445821952 | bytes 61766956 | solution.py:130
  1005.5 11.7 %fusion.4 = f32[64,4608]{1,0:T(8,128)S(1)} fusion(bf16[3072,4608]{1,0:T(8,128)(2,1)} %get-tuple-element.298, f32[64,3072]{1,0:T(8,128)S(1)} %mul.195, f32[64,3072]{1,0:T(8,128)S(1)} %sub.48, f32[64]{0:T(128)S(1)} %get-tuple-element.340, f32[3072]{0:T(1024)S(1)} %bitcast.70, f32[3072]{0:T(1024)S(1)} %bitcast.71, bf16[64,3072]{1,0:T(8,128)(2,1)S(1)} %get-tuple-element.292), kind=kOutput, calls=%fused_computation.17 | convolution fusion | flops 1813315584 | bytes 31482112 | tf_op jit(solution)/shard_map/while/body/eval_jaxpr/cond/branch_1_fun/dot_general | solution.py:50
  1021.7 5.5 fusion
  1027.2 1.9 collective-permute-start
  1031.0 5.3 collective-permute-done
  1036.3 1.0 bitcast_select_fusion.3
  1037.4 23.2 %collective-permute-start = (bf16[64,3072]{1,0:T(8,128)(2,1)S(1)}, bf16[64,3072]{1,0:T(8,128)(2,1)S(1)}, u32[]{:S(2)}, u32[]{:S(2)}) collective-permute-start(bf16[64,3072]{1,0:T(8,128)(2,1)S(1)} %get-tuple-element.476), channel_id=1, source_target_pairs={{0,1},{1,2},{2,3},{4,5},{5,6},{6,7},{8,9},{9,10},{10,11},{12,13},{... | collective-permute-start | bytes 1179656 | tf_op jit(solution)/shard_map/while/body/eval_jaxpr/ppermute | solution.py:22
  (332 shorter events, 102.8 us)
Async XLA Ops:
  6.5 543.0 %all-gather.3.cloned.1.call-start = ((), (), s32[]{:S(2)}) async-start(), calls=%async_computation | async-start | bytes 31850496 | tf_op jit(solution)/shard_map/all_gather | solution.py:100
  7.3 2.6 copy-start.4
  7.3 5.4 copy-start.2
  7.3 6.2 copy-start.3
  7.3 682.5 %all-gather.5.cloned.1.call-start = ((), (), s32[]{:S(2)}) async-start(), calls=%async_computation.1 | async-start | bytes 10616832 | tf_op jit(solution)/shard_map/all_gather | solution.py:104
  695.7 1.7 copy-start.1
  697.3 9.1 collective-permute-start.1
  707.5 33.4 %collective-permute-start = (bf16[64,3072]{1,0:T(8,128)(2,1)S(1)}, bf16[64,3072]{1,0:T(8,128)(2,1)S(1)}, u32[]{:S(2)}, u32[]{:S(2)}) collective-permute-start(bf16[64,3072]{1,0:T(8,128)(2,1)S(1)} %get-tuple-element.476), channel_id=1, source_target_pairs={{0,1},{1,2},{2,3},{4,5},{5,6},{6,7},{8,9},{9,10},{10,11},{12,13},{... | collective-permute-start | bytes 1179656 | tf_op jit(solution)/shard_map/while/body/eval_jaxpr/ppermute | solution.py:22
  758.7 1.0 copy-start
  768.7 9.1 collective-permute-start
  795.6 1.0 copy-start
  805.6 9.1 collective-permute-start
  832.6 1.0 copy-start
  842.6 9.1 collective-permute-start
  869.5 1.0 copy-start
  879.5 9.1 collective-permute-start
  906.4 1.0 copy-start
  916.4 9.1 collective-permute-start
  943.3 1.0 copy-start
  953.3 9.1 collective-permute-start
  980.3 1.0 copy-start
  990.3 9.1 collective-permute-start
  1017.2 1.0 copy-start
  1027.2 9.1 collective-permute-start
  1037.4 25.1 %collective-permute-start = (bf16[64,3072]{1,0:T(8,128)(2,1)S(1)}, bf16[64,3072]{1,0:T(8,128)(2,1)S(1)}, u32[]{:S(2)}, u32[]{:S(2)}) collective-permute-start(bf16[64,3072]{1,0:T(8,128)(2,1)S(1)} %get-tuple-element.476), channel_id=1, source_target_pairs={{0,1},{1,2},{2,3},{4,5},{5,6},{6,7},{8,9},{9,10},{10,11},{12,13},{... | collective-permute-start | bytes 1179656 | tf_op jit(solution)/shard_map/while/body/eval_jaxpr/ppermute | solution.py:22
Sparse Core Ops, SparseCore 0:
  8.9 540.6 all-gather.2
  551.7 138.0 all-gather.4
where the time goes:
time: 1070 us
  waiting for transfers between devices  740 us (69%)
  matrix products  167 us (16%)
  local copies, waits for them, and re-layouts  61 us (6%)
  other arithmetic  43.5 us (4%)
  starting transfers between devices  42.6 us (4%)
  between operations  13.7 us (1%)
    all_gather x1, waiting for transfers between devices, local(): qkv_all = lax.all_gather(w_qkv, 'dp', axis=1, tiled=True)  534 us
    all_gather x1, waiting for transfers between devices, local(): shard_rows = lax.all_gather(w_out, 'dp', axis=1, tiled=True)  126 us
    dot_general x9, matrix products, attend(): projected = jnp.dot(normed, qkv_weight, preferred_element_type=jnp.float32)  105 us
    ppermute x11, waiting for transfers between devices, passed_along(): lax.ppermute(value, axis, [(source, source + steps) for source in range(f...  78.9 us
    dot_general x8, matrix products, finish(): branch = jnp.dot(attended, out_weight, preferred_element_type=jnp.float32)  44 us
    ppermute x11, starting transfers between devices, passed_along(): lax.ppermute(value, axis, [(source, source + steps) for source in range(f...  42.6 us
  transfers between devices with their start and end apart: 13, of which 12 were waited for; matrix products, arithmetic and copies ran while one was open for 4% of the time, Pallas kernels for 0%

commit v1 on v0

v1 whole, which is shorter than its diff:
```python
import functools
import math

import jax
import jax.numpy as jnp
from jax import lax
from jax.experimental import pallas as pl
from jax.experimental.pallas import tpu as pltpu
from jax.sharding import PartitionSpec as P

HD = 64
GROUPS = 32
LANES = 128
WIDE = 256
PAIR = 2
MESH = pl.DeviceIdType.MESH
norm_eps = 1e-05


def pieces(rows):
    sixth = rows // 6
    return [(0, sixth, True), (sixth, 3 * sixth, False), (4 * sixth, 2 * sixth, False)]


def gather_events(nz, nx):
    events = []
    for dz in range(1 - nz, nz):
        for dx in range(1 - nx, nx):
            for piece in range(3):
                events.append((dz, dx, piece))
    return events


def next_hops(dz, dx, x_first, nz, nx):
    hops = []
    along_z = [1, -1] if dz == 0 else [1 if dz > 0 else -1]
    along_x = [1, -1] if dx == 0 else [1 if dx > 0 else -1]
    if x_first:
        if dz == 0:
            hops += [(0, step) for step in along_x if abs(dx + step) < nx]
        hops += [(step, 0) for step in along_z if abs(dz + step) < nz]
    else:
        if dx == 0:
            hops += [(step, 0) for step in along_z if abs(dz + step) < nz]
        hops += [(0, step) for step in along_x if abs(dx + step) < nx]
    return hops


def gather_kernel(nz, nx, qkv_ref, out_ref, qkv_full, out_full, send_sem, recv_sem, own_sem):
    me = lax.axis_index("dp")
    pipe = lax.axis_index("pipe")
    z = me // nx
    x = me % nx

    def inside(oz, ox):
        conds = []
        if oz > 0:
            conds.append(z + oz < nz)
        if oz < 0:
            conds.append(z + oz >= 0)
        if ox > 0:
            conds.append(x + ox < nx)
        if ox < 0:
            conds.append(x + ox >= 0)
        return functools.reduce(jnp.logical_and, conds) if conds else None

    def guarded(cond, body):
        if cond is None:
            body()
        else:
            pl.when(cond)(body)

    barrier = pltpu.get_barrier_semaphore()
    neighbours = [(1, 0), (-1, 0), (0, 1), (0, -1)]
    for oz, ox in neighbours:

        def greet(oz=oz, ox=ox):
            pl.semaphore_signal(
                barrier, inc=1, device_id=(me + oz * nx + ox, pipe), device_id_type=MESH
            )

        guarded(inside(oz, ox), greet)
    before = (z + nz - 1) // nz + (x + nx - 1) // nx
    after = (2 * nz - 2 - z) // nz + (2 * nx - 2 - x) // nx
    pl.semaphore_wait(barrier, before + after)

    arrays = [(qkv_ref, qkv_full), (out_ref, out_full)]
    events = gather_events(nz, nx)
    number = {event: at for at, event in enumerate(events)}

    def copy_to(event, hop, which):
        dz, dx, piece = event
        oz, ox = hop
        shard, full = arrays[which]
        rows = shard.shape[0]
        start, size, _ = pieces(rows)[piece]
        source = me - dz * nx - dx
        here = pl.ds(pl.multiple_of(source * rows + start, 16), size)
        src = shard.at[pl.ds(start, size)] if (dz, dx) == (0, 0) else full.at[here]
        slot = number[(dz + oz, dx + ox, piece)]
        return pltpu.make_async_remote_copy(
            src_ref=src,
            dst_ref=full.at[here],
            send_sem=send_sem.at[which, slot],
            recv_sem=recv_sem.at[which, slot],
            device_id=(me + oz * nx + ox, pipe),
            device_id_type=MESH,
        )

    def arrival(event, which):
        dz, dx, piece = event
        shard, full = arrays[which]
        rows = shard.shape[0]
        start, size, _ = pieces(rows)[piece]
        here = full.at[pl.ds(pl.multiple_of((me - dz * nx - dx) * rows + start, 16), size)]
        return pltpu.make_async_copy(here, here, recv_sem.at[which, number[event]])

    own = []
    for which, (shard, full) in enumerate(arrays):
        rows = shard.shape[0]
        own.append(
            pltpu.make_async_copy(
                shard, full.at[pl.ds(pl.multiple_of(me * rows, 16), rows)], own_sem.at[which]
            )
        )

    def order(event):
        dz, dx, piece = event
        x_first = pieces(6)[piece][2]
        leaf = not next_hops(dz, dx, x_first, nz, nx)
        return (leaf, abs(dz) + abs(dx), abs(dx) if not x_first else 0, piece)

    for event in sorted(events, key=order):
        dz, dx, piece = event
        hops = next_hops(dz, dx, pieces(6)[piece][2], nz, nx)

        def work(event=event, hops=hops):
            for which in range(2):
                if event[:2] != (0, 0):
                    arrival(event, which).wait()
                for hop in hops:
                    guarded(inside(*hop), lambda: copy_to(event, hop, which).start())

        guarded(inside(-dz, -dx), work)
        if event[:2] == (0, 0) and piece == 2:
            for copy in own:
                copy.start()
    for copy in own:
        copy.wait()
    for event in events:
        dz, dx, piece = event
        hops = next_hops(dz, dx, pieces(6)[piece][2], nz, nx)

        def finish(event=event, hops=hops):
            for which in range(2):
                for hop in hops:
                    guarded(inside(*hop), lambda: copy_to(event, hop, which).wait_send())

        if hops:
            guarded(inside(-dz, -dx), finish)


def gathered(qkv, out, nz, nx):
    slots = len(gather_events(nz, nx))
    count = nz * nx
    return pl.pallas_call(
        functools.partial(gather_kernel, nz, nx),
        out_shape=[
            jax.ShapeDtypeStruct((count * qkv.shape[0], qkv.shape[1]), qkv.dtype),
            jax.ShapeDtypeStruct((count * out.shape[0], out.shape[1]), out.dtype),
        ],
        in_specs=[pl.BlockSpec(memory_space=pl.ANY)] * 2,
        out_specs=[pl.BlockSpec(memory_space=pl.ANY)] * 2,
        scratch_shapes=[
            pltpu.SemaphoreType.DMA((2, slots)),
            pltpu.SemaphoreType.DMA((2, slots)),
            pltpu.SemaphoreType.DMA((2,)),
        ],
        compiler_params=pltpu.CompilerParams(collective_id=0, has_side_effects=True),
        name="gather_weights",
    )(qkv, out)


def split_dot(value, ones, parts):
    total = None
    for _ in range(parts):
        high = value.astype(jnp.bfloat16)
        term = jnp.dot(high, ones, preferred_element_type=jnp.float32)
        total = term if total is None else total + term
        value = value - high.astype(jnp.float32)
    return total


def layer_kernel(
    steps, group_width, x_ref, allowed_ref, keep_ref, gain_ref, bias_ref, group_ref, spread_ref,
    heads_ref, wq_ref, wk_ref, wv_ref, wo_ref, result_ref, normed_ref, total_ref,
):
    step = pl.program_id(0)
    rows = x_ref.shape[0]
    allowed = allowed_ref[...]
    keep = keep_ref[...]

    @pl.when(step == 0)
    def _():
        group = group_ref[...]
        spread = spread_ref[...]
        count = jnp.maximum(jnp.sum(allowed, axis=1, keepdims=True) * group_width, 1.0)
        sums = jnp.dot(x_ref[...], group, preferred_element_type=jnp.float32)
        mean = jnp.dot(
            allowed, sums, precision=lax.Precision.HIGHEST, preferred_element_type=jnp.float32
        ) / count
        centred = x_ref[...].astype(jnp.float32) - split_dot(mean, spread, 3)
        squares = split_dot(centred * centred, group, 2)
        var = jnp.dot(
            allowed, squares, precision=lax.Precision.HIGHEST, preferred_element_type=jnp.float32
        ) / count
        scale = split_dot(lax.rsqrt(var + norm_eps), spread, 3)
        normed = (centred * scale * gain_ref[...] + bias_ref[...]) * keep
        normed_ref[...] = normed.astype(jnp.bfloat16)
        total_ref[...] = x_ref[...].astype(jnp.float32)

    normed = normed_ref[...]
    ones = heads_ref[...]

    def unit(w_ref):
        got = jnp.dot(normed, w_ref[...], preferred_element_type=jnp.float32)
        square = split_dot(got * got, ones, 2) * (1.0 / HD)
        return (got * lax.rsqrt(square + 1e-06)).astype(jnp.bfloat16)

    query = unit(wq_ref)
    key = unit(wk_ref)
    value = jnp.dot(normed, wv_ref[...], preferred_element_type=jnp.float32).astype(jnp.bfloat16)
    lane = lax.broadcasted_iota(jnp.int32, (rows, LANES), 1)
    low = lane < HD
    low_mask = jnp.where(low, 1.0, 0.0).astype(jnp.bfloat16)
    high_mask = jnp.where(low, 0.0, 1.0).astype(jnp.bfloat16)
    allowed_both = jnp.concatenate([allowed, allowed], axis=0)
    spare = 1.0 - jnp.concatenate([keep, keep], axis=0)
    attended = []
    for at in range(0, WIDE, LANES):
        q, k, v = (a[:, at : at + LANES] for a in (query, key, value))
        both = jnp.concatenate([q * low_mask, q * high_mask], axis=0)
        scores = lax.dot_general(
            both, k, (((1,), (1,)), ((), ())), preferred_element_type=jnp.float32
        ) * (1.0 / math.sqrt(HD))
        expo = jnp.exp(scores) * allowed_both
        probs = (expo / (jnp.sum(expo, axis=1, keepdims=True) + spare)).astype(jnp.bfloat16)
        mixed = jnp.dot(probs, v, preferred_element_type=jnp.float32)
        attended.append(jnp.where(low, mixed[:rows], mixed[rows:]).astype(jnp.bfloat16))
    attended = jnp.concatenate(attended, axis=1)
    total_ref[...] += jnp.dot(attended, wo_ref[...], preferred_element_type=jnp.float32)

    @pl.when(step == steps - 1)
    def _():
        result_ref[...] = total_ref[...].astype(jnp.bfloat16)


def layer(stream, allowed, keep, gain, bias, masks, qkv, out):
    rows, width = stream.shape
    inner = out.shape[0]
    steps = inner // WIDE
    group, spread, heads = masks

    def whole(array):
        return pl.BlockSpec(array.shape, lambda j: (0, 0))

    def columns(part):
        return pl.BlockSpec((width, WIDE), lambda j: (0, part * steps + j))

    small = [stream, allowed, keep, gain, bias, group, spread, heads]
    return pl.pallas_call(
        functools.partial(layer_kernel, steps, width // GROUPS),
        grid=(steps,),
        out_shape=jax.ShapeDtypeStruct((rows, width), jnp.bfloat16),
        in_specs=[whole(a) for a in small]
        + [columns(0), columns(1), columns(2), pl.BlockSpec((WIDE, width), lambda j: (j, 0))],
        out_specs=pl.BlockSpec((rows, width), lambda j: (0, 0)),
        scratch_shapes=[
            pltpu.VMEM((rows, width), jnp.bfloat16),
            pltpu.VMEM((rows, width), jnp.float32),
        ],
        compiler_params=pltpu.CompilerParams(vmem_limit_bytes=48 * 1024 * 1024),
        cost_estimate=pl.CostEstimate(
            flops=8 * rows * width * inner, bytes_accessed=8 * width * inner, transcendentals=0
        ),
        name="layer",
    )(*small, qkv, qkv, qkv, out)


def local(nz, nx, tokens, segments, keep_mask, norm_gain, norm_bias, w_qkv, w_out):
    section = lax.axis_index("pipe")
    sections = lax.axis_size("pipe")
    seqs, length, width = tokens.shape
    rows = PAIR * length
    micro = seqs // PAIR
    qkv, out = gathered(w_qkv[0], w_out[0], nz, nx)

    group = (
        jnp.arange(width)[:, None] // (width // GROUPS) == jnp.arange(LANES)[None, :]
    ).astype(jnp.bfloat16)
    heads = (
        jnp.arange(WIDE)[:, None] // HD == jnp.arange(WIDE)[None, :] // HD
    ).astype(jnp.bfloat16)
    masks = (group, group.T, heads)

    kept = keep_mask.reshape(micro, rows) > 0
    images = segments.reshape(micro, rows)
    place = jnp.arange(rows) // length
    allowed = (
        (images[:, :, None] == images[:, None, :])
        & (place[:, None] == place[None, :])[None]
        & kept[:, :, None]
        & kept[:, None, :]
    ).astype(jnp.float32)
    keep = kept.astype(jnp.float32)[:, :, None]
    flat = tokens.reshape(micro, rows, width)

    incoming = jnp.zeros((rows, width), jnp.bfloat16)
    results = []
    ticks = micro + sections - 1
    for tick in range(ticks):
        index = jnp.clip(tick - section, 0, micro - 1)
        stream = jnp.where(section == 0, flat[min(tick, micro - 1)], incoming)
        result = layer(
            stream,
            lax.dynamic_index_in_dim(allowed, index, 0, keepdims=False),
            lax.dynamic_index_in_dim(keep, index, 0, keepdims=False),
            norm_gain,
            norm_bias,
            masks,
            qkv,
            out,
        )
        results.append(result)
        if tick < ticks - 1:
            incoming = lax.ppermute(
                result, "pipe", [(source, source + 1) for source in range(sections - 1)]
            )
    stacked = jnp.stack(results)
    mine = lax.dynamic_slice_in_dim(stacked, section, micro, 0)
    return mine.reshape(1, seqs, length, width)


def solution(mesh):
    placed = (
        P("dp", None, None),
        P("dp", None),
        P("dp", None),
        P("pipe", None),
        P("pipe", None),
        P("pipe", "dp", None),
        P("pipe", "dp", None),
    )
    nx = max(1, mesh.shape["pipe"] // 2)
    while mesh.shape["dp"] % nx:
        nx -= 1
    nz = mesh.shape["dp"] // nx
    return jax.shard_map(
        functools.partial(local, nz, nx),
        mesh=mesh,
        in_specs=placed,
        out_specs=P("pipe", "dp", None, None),
        check_vma=False,
    )
```

time: 1070 us -> 652 us (0.61)
  waiting for transfers between devices: 740 us -> 60 us
  Pallas kernels: 0 us -> 521 us
  matrix products: 167 us -> 0 us
  local copies, waits for them, and re-layouts: 61 us -> 17 us
  starting transfers between devices: 42.6 us -> 12.3 us
  between operations: 13.7 us -> 0.83 us
    all_gather x2 -> x0, waiting for transfers between devices: 660 us -> none  [the longest x1 534 us: local(): qkv_all = lax.all_gather(w_qkv, 'dp', axis=1, tiled=True)]
    pallas_call x0 -> x7, Pallas kernels: none -> 521 us  [the longest x1 383 us: gathered(): pl.pallas_call(functools.partial(gather_kernel, nz, nx), out_shape=[jax.S...]
    dot_general x72 -> x0, matrix products: 167 us -> none  [the longest x9 105 us: attend(): projected = jnp.dot(normed, qkv_weight, preferred_element_type=jnp.float32)]
    ppermute x11 -> x6, starting transfers between devices: 42.6 us -> 12.3 us  [local(): lax.ppermute(result, 'pipe', [(source, source + 1) for source in range(se...]
    pallas_call x0 -> x1, other arithmetic: none -> 22.5 us  [layer(): pl.pallas_call(functools.partial(layer_kernel, steps, width // GROUPS), g...]
    ppermute x11 -> x6, waiting for transfers between devices: 78.9 us -> 60 us  [local(): lax.ppermute(result, 'pipe', [(source, source + 1) for source in range(se...]
    reduce_sum x45 -> x0, other arithmetic: 14.9 us -> none  [the longest x9 5.68 us: group_normed(): jnp.sum(centred * centred, axis=2)]
  transfers between devices with their start and end apart: 13 -> 6, of which waited for: 12 -> 6; matrix products, arithmetic and copies ran while one was open for 4% -> 1% of each run, Pallas kernels for 0% -> 0%
where the time goes in v1:
time: 652 us; the launch traced here: 645 us
  Pallas kernels  521 us (80%)
  waiting for transfers between devices  60 us (9%)
  other arithmetic  34.3 us (5%)
  local copies, waits for them, and re-layouts  17 us (3%)
  starting transfers between devices  12.3 us (2%)
    pallas_call x1, Pallas kernels, gathered(): pl.pallas_call(functools.partial(gather_kernel, nz, nx), out_shape=[jax.S...  383 us
    pallas_call x6, Pallas kernels, layer(): pl.pallas_call(functools.partial(layer_kernel, steps, width // GROUPS), g...  138 us
    ppermute x6, waiting for transfers between devices, local(): lax.ppermute(result, 'pipe', [(source, source + 1) for source in range(se...  60 us
    pallas_call x1, other arithmetic, layer(): pl.pallas_call(functools.partial(layer_kernel, steps, width // GROUPS), g...  22.5 us
  transfers between devices with their start and end apart: 6, of which 6 were waited for; matrix products, arithmetic and copies ran while one was open for 1% of the time, Pallas kernels for 0%

profile of v1, /device:TPU:4, one launch (start us, length us, event | category | flops | bytes accessed | tf_op | source)
XLA Modules:
  0.0 645.0 jit_solution(2488781539310637723)
XLA Ops:
  0.0 1.4 fusion.group_ref
  1.4 0.2 fusion.1.spread_ref
  1.6 0.8 eq.183
  2.4 0.7 broadcast_compare_fusion.1
  3.0 0.1 gt.19
  3.1 0.1 broadcast_compare_fusion
  3.3 0.2 and_convert_fusion
  3.5 0.8 dynamic-slice_bitcast_fusion
  4.2 0.1 copy.8.keep_ref
  4.4 0.1 compare_convert_fusion.heads_ref
  4.5 0.0 copy-start.2
  4.5 0.0 copy-start.3
  4.5 3.3 fusion.12
  7.8 383.0 %gather_weights.1 = (bf16[3072,4608]{1,0:T(8,128)(2,1)}, bf16[1536,3072]{1,0:T(8,128)(2,1)}) custom-call(bf16[384,4608]{1,0:T(8,128)(2,1)} %bitcast.58, bf16[192,3072]{1,0:T(8,128)(2,1)} %bitcast.59), custom_call_target="tpu_custom_call" | custom-call | tf_op jit(solution)/shard_map/gather_weights/pallas_call | solution.py:166
  390.8 0.8 copy-done.7
  391.6 22.5 %layer.7 = bf16[128,3072]{1,0:T(8,128)(2,1)S(1)} custom-call(bf16[128,3072]{1,0:T(8,128)(2,1)S(1)} %bitcast.55, f32[128,128]{1,0:T(8,128)S(1)} %copy-done.7, f32[128,1]{1,0:T(8,128)S(1)} %copy.8.keep_ref, f32[1,3072]{1,0:T(1,128)S(1)} %copy-done.2, f32[1,3072]{1,0:T(1,128)S(1)} %copy-done.3, bf16[3072,128]{1,0:T(8,128)(2,1)S(1)} %fusion.group_ref, ...), custom_call_target="tpu_custom_call" | custom-call | flops 4831838208 | bytes 37748736 | tf_op jit(solution)/shard_map/layer/pallas_call | solution.py:271
  414.1 2.1 collective-permute-start
  416.2 0.1 copy.9.keep_ref
  416.3 11.1 %collective-permute-done = bf16[128,3072]{1,0:T(8,128)(2,1)S(1)} collective-permute-done((bf16[128,3072]{1,0:T(8,128)(2,1)S(1)}, bf16[128,3072]{1,0:T(8,128)(2,1)S(1)}, u32[]{:S(2)}, u32[]{:S(2)}) %collective-permute-start) | collective-permute-done | bytes 786464 | tf_op jit(solution)/shard_map/ppermute | solution.py:336
  427.4 1.2 bitcast_select_fusion.5.x_ref
  428.7 0.8 copy-done.6
  429.5 22.5 %layer.8 = bf16[128,3072]{1,0:T(8,128)(2,1)S(1)} custom-call(bf16[128,3072]{1,0:T(8,128)(2,1)S(1)} %bitcast_select_fusion.5.x_ref, f32[128,128]{1,0:T(8,128)S(1)} %copy-done.6, f32[128,1]{1,0:T(8,128)S(1)} %copy.9.keep_ref, f32[1,3072]{1,0:T(1,128)S(1)} %copy-done.2, f32[1,3072]{1,0:T(1,128)S(1)} %copy-done.3, bf16[3072,128]{1,0:T(8,128)(2,1)S(1)} %fusion.group_ref, ...), custom_call_target="tpu_custom_call" | custom-call | flops 4831838208 | bytes 37748736 | tf_op jit(solution)/shard_map/layer/pallas_call | solution.py:271
  452.0 1.9 collective-permute-start.1
  453.9 0.1 copy.10.keep_ref
  454.1 11.4 %collective-permute-done.1 = bf16[128,3072]{1,0:T(8,128)(2,1)} collective-permute-done((bf16[128,3072]{1,0:T(8,128)(2,1)S(1)}, bf16[128,3072]{1,0:T(8,128)(2,1)}, u32[]{:S(2)}, u32[]{:S(2)}) %collective-permute-start.1) | collective-permute-done | bytes 786464 | tf_op jit(solution)/shard_map/ppermute | solution.py:336
  465.4 1.5 bitcast_select_fusion.4.x_ref
  466.9 0.8 copy-done.5
  467.7 22.5 %layer.9 = bf16[128,3072]{1,0:T(8,128)(2,1)S(1)} custom-call(bf16[128,3072]{1,0:T(8,128)(2,1)S(1)} %bitcast_select_fusion.4.x_ref, f32[128,128]{1,0:T(8,128)S(1)} %copy-done.5, f32[128,1]{1,0:T(8,128)S(1)} %copy.10.keep_ref, f32[1,3072]{1,0:T(1,128)S(1)} %copy-done.2, f32[1,3072]{1,0:T(1,128)S(1)} %copy-done.3, bf16[3072,128]{1,0:T(8,128)(2,1)S(1)} %fusion.group_ref, ...), custom_call_target="tpu_custom_call" | custom-call | flops 4831838208 | bytes 37748736 | tf_op jit(solution)/shard_map/layer/pallas_call | solution.py:271
  490.2 2.1 collective-permute-start.2
  492.4 0.1 copy.11.keep_ref
  492.5 11.2 %collective-permute-done.2 = bf16[128,3072]{1,0:T(8,128)(2,1)} collective-permute-done((bf16[128,3072]{1,0:T(8,128)(2,1)S(1)}, bf16[128,3072]{1,0:T(8,128)(2,1)}, u32[]{:S(2)}, u32[]{:S(2)}) %collective-permute-start.2) | collective-permute-done | bytes 786464 | tf_op jit(solution)/shard_map/ppermute | solution.py:336
  503.6 1.5 bitcast_select_fusion.3.x_ref
  505.1 23.4 %layer.10 = bf16[128,3072]{1,0:T(8,128)(2,1)} custom-call(bf16[128,3072]{1,0:T(8,128)(2,1)S(1)} %bitcast_select_fusion.3.x_ref, f32[128,128]{1,0:T(8,128)S(1)} %get-tuple-element.16.allowed_ref, f32[128,1]{1,0:T(8,128)S(1)} %copy.11.keep_ref, f32[1,3072]{1,0:T(1,128)S(1)} %copy-done.2, f32[1,3072]{1,0:T(1,128)S(1)} %copy-done.3, ...), custom_call_target="tpu_custom_call" | custom-call | flops 4831838208 | bytes 37748736 | tf_op jit(solution)/shard_map/layer/pallas_call | solution.py:271
  528.5 1.9 collective-permute-start.3
  530.4 0.0 copy-done.1
  530.4 1.0 bitcast_dynamic-update-slice_fusion.6
  531.4 0.1 copy.12.keep_ref
  531.5 0.1 copy.13.keep_ref
  531.6 0.7 copy.14
  532.4 0.9 bitcast_dynamic-update-slice_fusion.5
  533.3 8.8 %collective-permute-done.3 = bf16[128,3072]{1,0:T(8,128)(2,1)} collective-permute-done((bf16[128,3072]{1,0:T(8,128)(2,1)}, bf16[128,3072]{1,0:T(8,128)(2,1)}, u32[]{:S(2)}, u32[]{:S(2)}) %collective-permute-start.3) | collective-permute-done | bytes 786464 | tf_op jit(solution)/shard_map/ppermute | solution.py:336
  542.1 1.5 bitcast_select_fusion.2.x_ref
  543.6 0.8 copy-done.4
  544.4 22.5 %layer.11 = bf16[128,3072]{1,0:T(8,128)(2,1)S(1)} custom-call(bf16[128,3072]{1,0:T(8,128)(2,1)S(1)} %bitcast_select_fusion.2.x_ref, f32[128,128]{1,0:T(8,128)S(1)} %copy-done.4, f32[128,1]{1,0:T(8,128)S(1)} %copy.12.keep_ref, f32[1,3072]{1,0:T(1,128)S(1)} %copy-done.2, f32[1,3072]{1,0:T(1,128)S(1)} %copy-done.3, bf16[3072,128]{1,0:T(8,128)(2,1)S(1)} %fusion.group_ref, ...), custom_call_target="tpu_custom_call" | custom-call | flops 4831838208 | bytes 37748736 | tf_op jit(solution)/shard_map/layer/pallas_call | solution.py:271
  567.0 2.2 collective-permute-start.4
  569.2 1.0 bitcast_dynamic-update-slice_fusion.4
  570.1 2.1 bitcast_dynamic-update-slice_fusion.3
  572.2 8.1 %collective-permute-done.4 = bf16[128,3072]{1,0:T(8,128)(2,1)S(1)} collective-permute-done((bf16[128,3072]{1,0:T(8,128)(2,1)S(1)}, bf16[128,3072]{1,0:T(8,128)(2,1)S(1)}, u32[]{:S(2)}, u32[]{:S(2)}) %collective-permute-start.4) | collective-permute-done | bytes 786464 | tf_op jit(solution)/shard_map/ppermute | solution.py:336
  580.3 0.0 copy-done.8
  580.3 0.1 bitcast_select_fusion.1.x_ref
  580.4 0.0 slice-start
  580.4 0.0 slice-start.1
  580.5 0.0 slice-start.2
  580.5 24.2 %layer.12 = bf16[128,3072]{1,0:T(8,128)(2,1)S(1)} custom-call(bf16[128,3072]{1,0:T(8,128)(2,1)S(1)} %bitcast_select_fusion.1.x_ref, f32[128,128]{1,0:T(8,128)S(1)} %get-tuple-element.14.allowed_ref, f32[128,1]{1,0:T(8,128)S(1)} %copy.13.keep_ref, f32[1,3072]{1,0:T(1,128)S(1)} %copy-done.2, f32[1,3072]{1,0:T(1,128)S(1)} %copy-done.3, ...), custom_call_target="tpu_custom_call" | custom-call | flops 4831838208 | bytes 37748736 | tf_op jit(solution)/shard_map/layer/pallas_call | solution.py:271
  604.7 2.1 collective-permute-start.5
  606.7 1.0 bitcast_dynamic-update-slice_fusion.2
  607.7 0.9 bitcast_dynamic-update-slice_fusion.1
  608.6 9.5 %collective-permute-done.5 = bf16[128,3072]{1,0:T(8,128)(2,1)S(1)} collective-permute-done((bf16[128,3072]{1,0:T(8,128)(2,1)S(1)}, bf16[128,3072]{1,0:T(8,128)(2,1)S(1)}, u32[]{:S(2)}, u32[]{:S(2)}) %collective-permute-start.5) | collective-permute-done | bytes 786464 | tf_op jit(solution)/shard_map/ppermute | solution.py:336
  618.1 0.1 bitcast_select_fusion
  618.3 0.0 slice-done
  618.3 0.0 slice-done.1
  618.3 0.0 slice-done.2
  618.3 22.5 %layer.13 = bf16[7,128,3072]{2,1,0:T(8,128)(2,1)} fusion(bf16[7,128,3072]{2,1,0:T(8,128)(2,1)} %bitcast_dynamic-update-slice_fusion.1, bf16[128,3072]{1,0:T(8,128)(2,1)S(1)} %bitcast_select_fusion, f32[128,128]{1,0:T(8,128)S(1)} %copy-done.10, f32[128,1]{1,0:T(8,128)S(1)} %copy-done.9, f32[1,3072]{1,0:T(1,128)S(1)} %copy-done.2, ...), kind=kCustom, calls=%fused_computation.4 | custom fusion | flops 4831838208 | bytes 41116160 | tf_op jit(solution)/shard_map/layer/pallas_call | solution.py:271
  640.8 3.8 constant_dynamic-slice_fusion
  (20 shorter events, 0.1 us)
Async XLA Ops:
  4.5 386.3 %copy-start.2 = (f32[1,3072]{1,0:T(1,128)S(1)}, f32[1,3072]{1,0:T(1,128)}, u32[]{:S(2)}) copy-start(f32[1,3072]{1,0:T(1,128)} %gain_ref.12) | copy-start | bytes 36868
  4.5 386.3 %copy-start.3 = (f32[1,3072]{1,0:T(1,128)S(1)}, f32[1,3072]{1,0:T(1,128)}, u32[]{:S(2)}) copy-start(f32[1,3072]{1,0:T(1,128)} %bias_ref.12) | copy-start | bytes 36868
  390.8 0.8 copy-start.7
  414.1 37.9 %copy-start = (bf16[128,3072]{1,0:T(8,128)(2,1)}, bf16[128,3072]{1,0:T(8,128)(2,1)S(1)}, u32[]{:S(2)}) copy-start(bf16[128,3072]{1,0:T(8,128)(2,1)S(1)} %layer.7) | copy-start | bytes 2359300
  414.1 13.3 %collective-permute-start = (bf16[128,3072]{1,0:T(8,128)(2,1)S(1)}, bf16[128,3072]{1,0:T(8,128)(2,1)S(1)}, u32[]{:S(2)}, u32[]{:S(2)}) collective-permute-start(bf16[128,3072]{1,0:T(8,128)(2,1)S(1)} %layer.7), channel_id=1, source_target_pairs={{0,1},{1,2},{2,3},{4,5},{5,6},{6,7},{8,9},{9,10},{10,11},{12,13},{... | collective-permute-start | bytes 2359304 | tf_op jit(solution)/shard_map/ppermute | solution.py:336
  428.7 0.8 copy-start.6
  452.0 13.4 %collective-permute-start.1 = (bf16[128,3072]{1,0:T(8,128)(2,1)S(1)}, bf16[128,3072]{1,0:T(8,128)(2,1)}, u32[]{:S(2)}, u32[]{:S(2)}) collective-permute-start(bf16[128,3072]{1,0:T(8,128)(2,1)S(1)} %layer.8), channel_id=1, source_target_pairs={{0,1},{1,2},{2,3},{4,5},{5,6},{6,7},{8,9},{9,10},{10,11},{12,13},{... | collective-permute-start | bytes 2359304 | tf_op jit(solution)/shard_map/ppermute | solution.py:336
  466.9 0.8 copy-start.5
  490.2 13.4 %collective-permute-start.2 = (bf16[128,3072]{1,0:T(8,128)(2,1)S(1)}, bf16[128,3072]{1,0:T(8,128)(2,1)}, u32[]{:S(2)}, u32[]{:S(2)}) collective-permute-start(bf16[128,3072]{1,0:T(8,128)(2,1)S(1)} %layer.9), channel_id=1, source_target_pairs={{0,1},{1,2},{2,3},{4,5},{5,6},{6,7},{8,9},{9,10},{10,11},{12,13},{... | collective-permute-start | bytes 2359304 | tf_op jit(solution)/shard_map/ppermute | solution.py:336
  505.1 25.4 %copy-start.1 = (bf16[128,3072]{1,0:T(8,128)(2,1)S(1)}, bf16[128,3072]{1,0:T(8,128)(2,1)}, u32[]{:S(2)}) copy-start(bf16[128,3072]{1,0:T(8,128)(2,1)} %copy-done) | copy-start | bytes 2359300
  528.5 13.6 %collective-permute-start.3 = (bf16[128,3072]{1,0:T(8,128)(2,1)}, bf16[128,3072]{1,0:T(8,128)(2,1)}, u32[]{:S(2)}, u32[]{:S(2)}) collective-permute-start(bf16[128,3072]{1,0:T(8,128)(2,1)} %layer.10), channel_id=1, source_target_pairs={{0,1},{1,2},{2,3},{4,5},{5,6},{6,7},{8,9},{9,10},{10,11},{12,13},{... | collective-permute-start | bytes 2359304 | tf_op jit(solution)/shard_map/ppermute | solution.py:336
  543.6 0.8 copy-start.4
  544.4 35.9 %copy-start.8 = (bf16[2,64,3072]{2,1,0:T(8,128)(2,1)S(1)}, bf16[2,64,3072]{2,1,0:T(8,128)(2,1)}, u32[]{:S(2)}) copy-start(bf16[2,64,3072]{2,1,0:T(8,128)(2,1)} %get-tuple-element.9) | copy-start | bytes 2359300
  567.0 13.3 %collective-permute-start.4 = (bf16[128,3072]{1,0:T(8,128)(2,1)S(1)}, bf16[128,3072]{1,0:T(8,128)(2,1)S(1)}, u32[]{:S(2)}, u32[]{:S(2)}) collective-permute-start(bf16[128,3072]{1,0:T(8,128)(2,1)S(1)} %layer.11), channel_id=1, source_target_pairs={{0,1},{1,2},{2,3},{4,5},{5,6},{6,7},{8,9},{9,10},{10,11},{12,13},{... | collective-permute-start | bytes 2359304 | tf_op jit(solution)/shard_map/ppermute | solution.py:336
  580.4 37.8 %slice-start = ((s8[9437184]{0:T(1024)(128)(4,1)}), s8[4194304]{0:T(1024)(128)(4,1)S(1)}, s32[]{:S(2)}) async-start(s8[9437184]{0:T(1024)(128)(4,1)} %bitcast.56), calls=%async_computation | async-start | bytes 8388608
  580.4 37.8 %slice-start.1 = ((s8[9437184]{0:T(1024)(128)(4,1)}), s8[4194304]{0:T(1024)(128)(4,1)S(1)}, s32[]{:S(2)}) async-start(s8[9437184]{0:T(1024)(128)(4,1)} %bitcast.56), calls=%async_computation.1 | async-start | bytes 8388608
  580.5 37.8 %slice-start.2 = ((s8[9437184]{0:T(1024)(128)(4,1)}), s8[1048576]{0:T(1024)(128)(4,1)S(1)}, s32[]{:S(2)}) async-start(s8[9437184]{0:T(1024)(128)(4,1)} %bitcast.56), calls=%async_computation.2 | async-start | bytes 2097152
  604.7 13.6 %copy-start.9 = (f32[128,1]{1,0:T(8,128)S(1)}, f32[128,1]{1,0:T(8,128)}, u32[]{:S(2)}) copy-start(f32[128,1]{1,0:T(8,128)} %copy.14) | copy-start | bytes 1540
  604.7 13.6 %copy-start.10 = (f32[128,128]{1,0:T(8,128)S(1)}, f32[128,128]{1,0:T(8,128)}, u32[]{:S(2)}) copy-start(f32[128,128]{1,0:T(8,128)} %get-tuple-element.13) | copy-start | bytes 196612
  604.7 13.4 %collective-permute-start.5 = (bf16[128,3072]{1,0:T(8,128)(2,1)S(1)}, bf16[128,3072]{1,0:T(8,128)(2,1)S(1)}, u32[]{:S(2)}, u32[]{:S(2)}) collective-permute-start(bf16[128,3072]{1,0:T(8,128)(2,1)S(1)} %layer.12), channel_id=1, source_target_pairs={{0,1},{1,2},{2,3},{4,5},{5,6},{6,7},{8,9},{9,10},{10,11},{12,13},{... | collective-permute-start | bytes 2359304 | tf_op jit(solution)/shard_map/ppermute | solution.py:336
